TPU v7x, 32 devices: a whole 2x2x4 slice. The times are simulated.
32 devices in a mesh: exp: 8 (over y, x, core), rep: 4 (over z).
Axes of the slice: x: 2, y: 2, z: 4, core: 2. Of those that a mesh axis runs over, the one named last changes fastest.
Arguments:
- tokens: bfloat16 [256, 6144], P(('exp', 'rep')), may hold values from -6 to 6
- slot_index: int32 [256], P(('exp', 'rep')), may hold values from 0 to 2, as said below
- saved_inputs: bfloat16 [4, 512, 6144], P('rep'), may hold values from -6 to 6
- cotangents: bfloat16 [4, 512, 2, 8192], P('rep', None, None, 'exp'), may hold values from -0.046875 to 0.046875
- master: float32 [6144, 2, 8192], P('rep', None, 'exp'), may hold values from -0.078125 to 0.078125
- moment1: float32 [6144, 2, 8192], P('rep', None, 'exp'), may hold values from -0.046875 to 0.046875
- moment2: float32 [6144, 2, 8192], P('rep', None, 'exp'), may hold values from 3e-07 to 3e-05
Outputs:
- new_master: float32 [6144, 2, 8192], P('rep', None, 'exp')
- new_moment1: float32 [6144, 2, 8192], P('rep', None, 'exp')
- new_moment2: float32 [6144, 2, 8192], P('rep', None, 'exp')
- hidden: bfloat16 [4, 16, 8192], P('rep', None, 'exp')
Inputs may be any that keep to these rules, and one draw needn't show every extreme that they name: `slot_index`: in each aligned block of 8 tokens every slot 0 to 1 is held by exactly one token; the other tokens carry 2, meaning not routed to this expert.
All inputs are finite; a program needn't handle non-finite values.
Results may differ from a plain program's by a relative error of at most 0.0075.
Values may be sent and summed in bfloat16 or wider, within the bound.
A program may use at most 192 MiB of HBM per device.

v0:
```python
import jax
import jax.numpy as jnp
from jax import lax
from jax.sharding import PartitionSpec as P

STEP = 100


def shards(tokens, slot_index, saved_inputs, cotangents, master, moment1, moment2):
    replicas = lax.axis_size("rep")
    rows_in = saved_inputs[0]
    cotangent = cotangents[0]
    hidden_dev = cotangent.shape[2]
    cot_flat = cotangent.reshape(cotangent.shape[0], 2 * hidden_dev)
    feature_width = rows_in.shape[1]
    row_share = feature_width // replicas
    contract_rows = (((0,), (0,)), ((), ()))
    summed = lax.psum_scatter(
        lax.dot_general(
            rows_in, cot_flat, contract_rows, preferred_element_type=jnp.float32
        ).astype(jnp.bfloat16),
        "rep",
        scatter_dimension=0,
        tiled=True,
    ).astype(jnp.float32)
    average = summed.reshape(row_share, 2, hidden_dev) / replicas
    new_first = 0.9 * moment1 + 0.1 * average
    new_second = 0.999 * moment2 + 0.001 * average * average
    correct_one = 1.0 - 0.9**STEP
    correct_two = 1.0 - 0.999**STEP
    ratio = new_first / correct_one / (jnp.sqrt(new_second / correct_two) + 1e-08)
    new_master = master - 0.001 * (ratio + 0.1 * master)
    own_weights = new_master.astype(jnp.bfloat16)
    capacity = tokens.shape[0] // 4
    onehot = (slot_index[:, None] == jnp.arange(capacity, dtype=jnp.int32)[None, :]).astype(
        jnp.bfloat16
    )
    chosen = lax.dot_general(
        onehot, tokens, contract_rows, preferred_element_type=jnp.float32
    ).astype(jnp.bfloat16)
    routed = lax.all_gather(chosen, "exp", axis=0, tiled=True)
    pieces = lax.all_to_all(routed, "rep", split_axis=1, concat_axis=0, tiled=True)
    local_weights = own_weights.reshape(row_share, 2 * hidden_dev)
    preact = lax.psum_scatter(
        jnp.dot(pieces, local_weights, preferred_element_type=jnp.float32),
        "rep",
        scatter_dimension=0,
        tiled=True,
    )
    preact = preact.reshape(routed.shape[0], 2, hidden_dev)
    hidden = (jax.nn.silu(preact[:, 0]) * preact[:, 1]).astype(jnp.bfloat16)
    return (new_master, new_first, new_second, hidden[None])


def solution(mesh):
    return jax.shard_map(
        shards,
        mesh=mesh,
        in_specs=(
            P(("exp", "rep"), None),
            P(("exp", "rep")),
            P("rep", None, None),
            P("rep", None, None, "exp"),
            P("rep", None, "exp"),
            P("rep", None, "exp"),
            P("rep", None, "exp"),
        ),
        out_specs=(
            P("rep", None, "exp"),
            P("rep", None, "exp"),
            P("rep", None, "exp"),
            P("rep", None, "exp"),
        ),
        check_vma=False,
    )
```

profile of v0, /device:TPU:0, one launch (start us, length us, event | category | flops | bytes accessed | tf_op | source)
XLA Modules:
  0.0 587.3 jit_solution(17405768758187488058)
XLA Ops:
  7.2 0.0 copy-start
  7.2 0.0 reduce-scatter.3.cloned.1.call-start
  7.2 2.2 copy.26
  9.4 19.5 %convolution_convert_fusion = bf16[6144,2048]{1,0:T(8,128)(2,1)} fusion(bf16[512,2048]{1,0:T(8,128)(2,1)S(1)} %bitcast.30, bf16[1,512,6144]{2,1,0:T(8,128)(2,1)} %param.9), kind=kOutput, calls=%fused_computation | convolution fusion | flops 12897484800 | bytes 33554432 | tf_op jit(solution)/shard_map/dot_general | solution.py:19
  28.9 0.0 copy-start.2
  28.9 0.0 reduce-scatter.3.cloned.1.call-update
  28.9 0.0 copy-done
  28.9 0.6 copy-done.2
  29.5 0.3 fusion.1
  29.8 10.7 %all-gather = bf16[8,2,6144]{2,1,0:T(2,128)(2,1)S(1)} all-gather(bf16[1,2,6144]{2,1,0:T(2,128)(2,1)S(1)} %fusion.1), channel_id=1, replica_groups=mesh['exp'=8,'rep'=4] {'exp'}, dimensions={0}, use_global_device_ids=true | all-gather | bytes 221184 | tf_op jit(solution)/shard_map/all_gather | solution.py:41
  40.6 0.1 all_to_all.14
  40.7 0.7 copy.21
  41.4 4.9 all-to-all-start
  46.3 0.0 reduce-scatter.5.cloned.1.call-start
  46.3 403.0 %reduce-scatter.3.cloned.1.call-done = bf16[1536,2048]{1,0:T(8,128)(2,1)} async-done(((bf16[6144,2048]{1,0:T(8,128)(2,1)}), bf16[1536,2048]{1,0:T(8,128)(2,1)}) %reduce-scatter.3.cloned.1.call-update) | async-done | bytes 6291472 | tf_op jit(solution)/shard_map/reduce_scatter | solution.py:18
  449.3 15.3 %fusion = (f32[1536,2048]{1,0:T(8,128)}, f32[1536,2048]{1,0:T(8,128)}) fusion(bf16[1536,2048]{1,0:T(8,128)(2,1)} %reduce-scatter.3.cloned.1.call-done), kind=kLoop, calls=%fused_computation.4 | loop fusion | flops 15728640 | bytes 31457280 | tf_op jit(solution)/shard_map/mul | solution.py:28
  464.7 16.9 %mul.63 = f32[1536,2,1024]{2,1,0:T(2,128)} reshape(f32[1536,2048]{1,0:T(8,128)} %get-tuple-element.9) | data formatting | bytes 25165824 | tf_op jit(solution)/shard_map/mul | solution.py:27
  481.5 16.9 %mul.69 = f32[1536,2,1024]{2,1,0:T(2,128)} reshape(f32[1536,2048]{1,0:T(8,128)} %get-tuple-element.8) | data formatting | bytes 25165824 | tf_op jit(solution)/shard_map/mul | solution.py:28
  498.4 0.0 copy-start.1
  498.4 46.6 %fusion.6 = (bf16[1536,2,1024]{2,1,0:T(2,128)(2,1)S(1)}, f32[1536,2,1024]{2,1,0:T(2,128)}, f32[1536,2,1024]{2,1,0:T(2,128)}, f32[1536,2,1024]{2,1,0:T(2,128)}) fusion(f32[1536,2,1024]{2,1,0:T(2,128)} %param.11, f32[1536,2,1024]{2,1,0:T(2,128)} %mul.63, f32[1536,2,1024]{2,1,0:T(2,128)} %param.12, f32[1536,2,1024]{2,1,0:T(2,128)} %mul.69, ...), kind=kLoop, calls=%fused_computation.17 | loop fusion | flops 40894464 | bytes 106954752 | tf_op jit(solution)/shard_map/convert_element_type | solution.py:33
  545.0 5.3 copy.27
  550.3 0.0 all-to-all-done
  550.3 4.8 fusion.8
  555.1 0.0 reduce-scatter.5.cloned.1.call-update
  555.2 23.6 %reduce-scatter.5.cloned.1.call-done = f32[16,2048]{1,0:T(8,128)} async-done(((f32[64,2048]{1,0:T(8,128)}), f32[16,2048]{1,0:T(8,128)}) %reduce-scatter.5.cloned.1.call-update) | async-done | bytes 131088 | tf_op jit(solution)/shard_map/reduce_scatter | solution.py:44
  578.7 1.0 reshape.68
  579.7 0.1 fusion.7
  579.8 0.7 fusion.4
  580.5 0.0 copy-done.1
Async XLA Ops:
  7.2 21.7 %copy-start = (bf16[8,6144]{1,0:T(8,128)(2,1)S(1)}, bf16[8,6144]{1,0:T(8,128)(2,1)}, u32[]{:S(2)}) copy-start(bf16[8,6144]{1,0:T(8,128)(2,1)} %param.7) | copy-start | bytes 294916
  7.2 442.1 %reduce-scatter.3.cloned.1.call-start = ((), (), s32[]{:S(2)}) async-start(), calls=%async_computation.3 | async-start | bytes 31457280 | tf_op jit(solution)/shard_map/reduce_scatter | solution.py:18
  28.9 0.7 copy-start.2
  41.4 508.9 %all-to-all-start = ((bf16[16,4,1536]{2,0,1:T(8,128)(2,1)}), bf16[16,4,1536]{2,0,1:T(8,128)(2,1)S(1)}, u32[]{:S(2)}, u32[]{:S(2)}) async-start(bf16[16,4,1536]{2,0,1:T(8,128)(2,1)} %copy.21), calls=%async_computation.1 | async-start | bytes 393216 | tf_op jit(solution)/shard_map/all_to_all | solution.py:42
  46.3 532.4 %reduce-scatter.5.cloned.1.call-start = ((), (), s32[]{:S(2)}) async-start(), calls=%async_computation.4 | async-start | bytes 655360 | tf_op jit(solution)/shard_map/reduce_scatter | solution.py:44
  498.4 82.1 %copy-start.1 = (bf16[8,6144]{1,0:T(8,128)(2,1)S(1)}, bf16[8,6144]{1,0:T(8,128)(2,1)}, u32[]{:S(2)}) copy-start(bf16[8,6144]{1,0:T(8,128)(2,1)} %param.7) | copy-start | bytes 294916
Sparse Core Ops, SparseCore 0:
  29.0 420.2 reduce-scatter.2
  555.3 23.3 reduce-scatter.4
where the time goes:
time: 588 us; the launch traced here: 587 us
  waiting for transfers between devices  427 us (73%)
  other arithmetic  62.6 us (11%)
  local copies, waits for them, and re-layouts  43.8 us (7%)
  matrix products  24.5 us (4%)
  between operations  14.1 us (2%)
  blocking collectives  10.7 us (2%)
    reduce_scatter x1, waiting for transfers between devices, shards(): lax.psum_scatter(lax.dot_general(rows_in, cot_flat, contract_rows, prefer...  403 us
    convert_element_type x1, other arithmetic, shards(): own_weights = new_master.astype(jnp.bfloat16)  46.6 us
    reduce_scatter x1, waiting for transfers between devices, shards(): lax.psum_scatter(jnp.dot(pieces, local_weights, preferred_element_type=jn...  23.6 us
    dot_general x1, matrix products, shards(): lax.dot_general(rows_in, cot_flat, contract_rows, preferred_element_type=...  19.5 us
    mul x1, local copies, waits for them, and re-layouts, shards(): new_first = 0.9 * moment1 + 0.1 * average  16.9 us
    mul x1, local copies, waits for them, and re-layouts, shards(): new_second = 0.999 * moment2 + 0.001 * average * average  16.9 us
    mul x1, other arithmetic, shards(): new_second = 0.999 * moment2 + 0.001 * average * average  15.3 us
  transfers between devices with their start and end apart: 3, of which 2 were waited for; matrix products, arithmetic and copies ran while one was open for 17% of the time, Pallas kernels for 0%

commit v1 on v0

v1 whole, which is shorter than its diff:
```python
import functools

import jax
import jax.numpy as jnp
from jax import lax
from jax.experimental import pallas as pl
from jax.experimental.pallas import tpu as pltpu
from jax.sharding import PartitionSpec as P

STEP = 100


def largest_block(size, most):
    block = most
    while size % block:
        block //= 2
    return block


def adam_kernel(replicas, passed, rows_ref, cot_ref, pieces_ref, master_ref, first_ref, second_ref, *rest):
    out_master, out_first, out_second, out_pre = rest[passed:]
    width = master_ref.shape[2]
    correct_one = 1.0 - 0.9**STEP
    correct_two = 1.0 - 0.999**STEP

    @pl.when(pl.program_id(0) == 0)
    def _():
        out_pre[...] = jnp.zeros_like(out_pre)

    for g in range(2):
        cols = slice(g * width, (g + 1) * width)
        total = jnp.dot(rows_ref[...], cot_ref[:, cols], preferred_element_type=jnp.float32)
        average = total / replicas
        new_first = 0.9 * first_ref[:, g, :] + 0.1 * average
        new_second = 0.999 * second_ref[:, g, :] + 0.001 * average * average
        ratio = new_first / correct_one / (jnp.sqrt(new_second / correct_two) + 1e-08)
        old = master_ref[:, g, :]
        new_master = old - 0.001 * (ratio + 0.1 * old)
        out_first[:, g, :] = new_first
        out_second[:, g, :] = new_second
        out_master[:, g, :] = new_master
        out_pre[:, cols] += jnp.dot(
            pieces_ref[...], new_master.astype(jnp.bfloat16), preferred_element_type=jnp.float32
        )


def adam_chunk(chunk, width, replicas, rows_t, cot, pieces, master, first, second, before):
    share, depth = rows_t.shape
    routed_rows = pieces.shape[0]
    block = largest_block(share, 256)
    state = pl.BlockSpec((block, 2, width), lambda i: (i, 0, chunk))
    shape = jax.ShapeDtypeStruct(master.shape, jnp.float32)
    passed = len(before)
    return pl.pallas_call(
        functools.partial(adam_kernel, replicas, passed),
        grid=(share // block,),
        in_specs=[
            pl.BlockSpec((block, depth), lambda i: (i, 0)),
            pl.BlockSpec((depth, 2 * width), lambda i: (0, 0)),
            pl.BlockSpec((routed_rows, block), lambda i: (0, i)),
            state,
            state,
            state,
        ]
        + [pl.BlockSpec(memory_space=pl.ANY)] * passed,
        out_specs=[state, state, state, pl.BlockSpec((routed_rows, 2 * width), lambda i: (0, 0))],
        out_shape=[shape, shape, shape, jax.ShapeDtypeStruct((routed_rows, 2 * width), jnp.float32)],
        input_output_aliases={6 + i: i for i in range(passed)},
        cost_estimate=pl.CostEstimate(
            flops=2 * share * depth * 2 * width,
            bytes_accessed=24 * share * 2 * width + 2 * share * depth,
            transcendentals=0,
        ),
        compiler_params=pltpu.CompilerParams(vmem_limit_bytes=40 * 1024 * 1024),
    )(rows_t, cot, pieces, master, first, second, *before)


def shards(tokens, slot_index, saved_inputs, cotangents, master, moment1, moment2):
    replicas = lax.axis_size("rep")
    peers = lax.axis_size("exp")
    rows_in = saved_inputs[0]
    saved, feature_width = rows_in.shape
    hidden_dev = cotangents.shape[3]
    row_share = feature_width // replicas
    contract_rows = (((0,), (0,)), ((), ()))

    capacity = tokens.shape[0] // 4
    onehot = (slot_index[:, None] == jnp.arange(capacity, dtype=jnp.int32)[None, :]).astype(
        jnp.bfloat16
    )
    chosen = lax.dot_general(
        onehot, tokens, contract_rows, preferred_element_type=jnp.float32
    ).astype(jnp.bfloat16)
    routed = lax.all_gather(chosen, "exp", axis=0, tiled=True)
    pieces = lax.all_to_all(routed, "rep", split_axis=1, concat_axis=0, tiled=True)

    part = saved // peers
    own = lax.dynamic_slice_in_dim(rows_in, lax.axis_index("exp") * part, part, 0)
    own = lax.all_to_all(own, "rep", split_axis=1, concat_axis=0, tiled=True)
    everyone = lax.all_gather(own, "exp", axis=0, tiled=True)
    everyone = everyone.reshape(peers, replicas, part, row_share)
    rows_t = everyone.transpose(3, 1, 0, 2).reshape(row_share, replicas * saved)

    width = max(128, hidden_dev // 4)
    outs = ()
    partials = []
    for chunk in range(hidden_dev // width):
        piece = cotangents[0, :, :, chunk * width : (chunk + 1) * width].reshape(saved, 2 * width)
        cot = lax.all_gather(piece, "rep", axis=0, tiled=True)
        *outs, pre = adam_chunk(
            chunk, width, replicas, rows_t, cot, pieces, master, moment1, moment2, tuple(outs)
        )
        partials.append(pre)
    preact = lax.psum_scatter(
        jnp.concatenate(partials, axis=1), "rep", scatter_dimension=0, tiled=True
    )
    preact = preact.reshape(routed.shape[0], hidden_dev // width, 2, width)
    hidden = (jax.nn.silu(preact[:, :, 0]) * preact[:, :, 1]).astype(jnp.bfloat16)
    return (*outs, hidden.reshape(1, routed.shape[0], hidden_dev))


def solution(mesh):
    return jax.shard_map(
        shards,
        mesh=mesh,
        in_specs=(
            P(("exp", "rep"), None),
            P(("exp", "rep")),
            P("rep", None, None),
            P("rep", None, None, "exp"),
            P("rep", None, "exp"),
            P("rep", None, "exp"),
            P("rep", None, "exp"),
        ),
        out_specs=(
            P("rep", None, "exp"),
            P("rep", None, "exp"),
            P("rep", None, "exp"),
            P("rep", None, "exp"),
        ),
        check_vma=False,
    )
```

time: 588 us -> 324 us (0.55)
  waiting for transfers between devices: 427 us -> 141 us
  Pallas kernels: 0 us -> 83.8 us
  other arithmetic: 62.6 us -> 1.49 us
  blocking collectives: 10.7 us -> 36.2 us
  matrix products: 24.5 us -> 0.29 us
    reduce_scatter x2 -> x1, waiting for transfers between devices: 427 us -> 20.5 us  [shards(): lax.psum_scatter(jnp.concatenate(partials, axis=1), 'rep', scatter_dimens...]
    all_gather x0 -> x5, waiting for transfers between devices: none -> 120 us  [the longest x4 95.7 us: shards(): cot = lax.all_gather(piece, 'rep', axis=0, tiled=True)]
    pallas_call x0 -> x4, Pallas kernels: none -> 83.8 us  [adam_chunk(): pl.pallas_call(functools.partial(adam_kernel, replicas, passed), grid=(sh...]
    convert_element_type x2 -> x1, other arithmetic: 47.3 us -> 0.65 us  [shards(): (jax.nn.silu(preact[:, :, 0]) * preact[:, :, 1]).astype(jnp.bfloat16)]
    mul x2 -> x0, local copies, waits for them, and re-layouts: 33.7 us -> none  [the longest x1 16.9 us: shards(): new_first = 0.9 * moment1 + 0.1 * average]
    all_to_all x0 -> x1, blocking collectives: none -> 26.3 us  [shards(): own = lax.all_to_all(own, 'rep', split_axis=1, concat_axis=0, tiled=True)]
    dot_general x2 -> x0, matrix products: 24.3 us -> none  [the longest x1 19.5 us: shards(): lax.dot_general(rows_in, cot_flat, contract_rows, preferred_element_type=...]
    mul x1 -> x0, other arithmetic: 15.3 us -> none  [shards(): new_second = 0.999 * moment2 + 0.001 * average * average]
  transfers between devices with their start and end apart: 3 -> 7, of which waited for: 2 -> 6; matrix products, arithmetic and copies ran while one was open for 17% -> 7% of each run, Pallas kernels for 0% -> 19%
where the time goes in v1:
time: 324 us; the launch traced here: 323 us
  waiting for transfers between devices  141 us (44%)
  Pallas kernels  83.8 us (26%)
  local copies, waits for them, and re-layouts  42.9 us (13%)
  blocking collectives  36.2 us (11%)
  between operations  14.2 us (4%)
  starting transfers between devices  3.61 us (1%)
    all_gather x4, waiting for transfers between devices, shards(): cot = lax.all_gather(piece, 'rep', axis=0, tiled=True)  95.7 us
    pallas_call x4, Pallas kernels, adam_chunk(): pl.pallas_call(functools.partial(adam_kernel, replicas, passed), grid=(sh...  83.8 us
    all_to_all x1, blocking collectives, shards(): own = lax.all_to_all(own, 'rep', split_axis=1, concat_axis=0, tiled=True)  26.3 us
    all_gather x1, waiting for transfers between devices, shards(): everyone = lax.all_gather(own, 'exp', axis=0, tiled=True)  24.4 us
    unnamed x26, local copies, waits for them, and re-layouts  21.1 us
    reduce_scatter x1, waiting for transfers between devices, shards(): lax.psum_scatter(jnp.concatenate(partials, axis=1), 'rep', scatter_dimens...  20.5 us
    all_gather x1, blocking collectives, shards(): routed = lax.all_gather(chosen, 'exp', axis=0, tiled=True)  9.91 us
    reshape x1, local copies, waits for them, and re-layouts, shards(): rows_t = everyone.transpose(3, 1, 0, 2).reshape(row_share, replicas * saved)  8.78 us
  transfers between devices with their start and end apart: 7, of which 6 were waited for; matrix products, arithmetic and copies ran while one was open for 7% of the time, Pallas kernels for 19%

profile of v1, /device:TPU:0, one launch (start us, length us, event | category | flops | bytes accessed | tf_op | source)
XLA Modules:
  0.0 323.2 jit_solution(12295160262048194604)
XLA Ops:
  7.2 0.0 all-gather.7.cloned.1.call-start
  7.2 1.2 constant_dynamic-slice_fusion
  8.4 0.6 all_to_all.28
  9.0 0.1 copy.34
  9.2 26.3 %all_to_all.38 = bf16[64,4,1536]{2,0,1:T(8,128)(2,1)} all-to-all(bf16[64,4,1536]{2,0,1:T(8,128)(2,1)S(1)} %copy.34), channel_id=1, replica_groups=mesh['exp'=8,'rep'=4] {'rep'}, dimensions={1} | all-to-all | bytes 1572864 | tf_op jit(solution)/shard_map/all_to_all | solution.py:99
  35.5 0.0 all-gather.7.cloned.1.call-update
  35.5 0.0 all-gather.15.cloned.1.call-start
  35.6 2.7 fusion.2
  38.2 0.9 copy.44
  39.1 0.0 all-gather.15.cloned.1.call-update
  39.1 0.0 all-gather.13.cloned.1.call-start
  39.2 0.9 copy.43
  40.1 0.0 all-gather.11.cloned.1.call-start
  40.2 0.9 copy.42
  41.1 0.0 all-gather.11.cloned.1.call-update
  41.1 0.0 all-gather.9.cloned.1.call-start
  41.2 0.9 copy.41
  42.1 0.3 fusion
  42.4 9.9 %all-gather = bf16[8,2,6144]{2,1,0:T(2,128)(2,1)S(1)} all-gather(bf16[1,2,6144]{2,1,0:T(2,128)(2,1)S(1)} %fusion), channel_id=1, replica_groups=mesh['exp'=8,'rep'=4] {'exp'}, dimensions={0}, use_global_device_ids=true | all-gather | bytes 221184 | tf_op jit(solution)/shard_map/all_gather | solution.py:94
  52.3 0.1 all_to_all.32
  52.5 0.7 copy.36
  53.2 3.4 %all-to-all-start.1 = ((bf16[16,4,1536]{2,0,1:T(8,128)(2,1)}), bf16[16,4,1536]{2,0,1:T(8,128)(2,1)S(1)}, u32[]{:S(2)}, u32[]{:S(2)}) async-start(bf16[16,4,1536]{2,0,1:T(8,128)(2,1)} %copy.36), calls=%async_computation.1 | async-start | bytes 393216 | tf_op jit(solution)/shard_map/all_to_all | solution.py:95
  56.5 0.0 reduce-scatter.2.cloned.1.call-start
  56.6 24.4 %all-gather.7.cloned.1.call-done = bf16[2048,1536]{1,0:T(8,128)(2,1)} async-done(((bf16[256,1536]{1,0:T(8,128)(2,1)}), bf16[2048,1536]{1,0:T(8,128)(2,1)}) %all-gather.7.cloned.1.call-update) | async-done | bytes 6291472 | tf_op jit(solution)/shard_map/all_gather | solution.py:100
  81.0 6.1 %copy.35 = bf16[1536,4,8,64]{0,3,2,1:T(8,128)(2,1)} copy(bf16[1536,4,8,64]{0,3,1,2:T(8,128)(2,1)} %bitcast.30) | data formatting | bytes 12582912 | tf_op jit(solution)/shard_map/transpose | solution.py:102
  87.1 8.8 %copy.40.rows_ref = bf16[1536,2048]{1,0:T(8,128)(2,1)} copy(bf16[1536,2048]{0,1:T(8,128)(2,1)} %bitcast.29) | data formatting | bytes 12582912 | tf_op jit(solution)/shard_map/reshape | solution.py:102
  95.9 33.2 %all-gather.15.cloned.1.call-done.cot_ref = bf16[2048,512]{1,0:T(8,128)(2,1)} async-done(((bf16[512,512]{1,0:T(8,128)(2,1)}), bf16[2048,512]{1,0:T(8,128)(2,1)}) %all-gather.15.cloned.1.call-update) | async-done | bytes 2097168 | tf_op jit(solution)/shard_map/all_gather | solution.py:109
  129.1 2.8 copy-done.2
  131.9 1.6 copy-done.6
  133.4 21.0 %shard_map.102 = (f32[1536,2,1024]{2,1,0:T(2,128)}, f32[1536,2,1024]{2,1,0:T(2,128)}, f32[1536,2,1024]{2,1,0:T(2,128)}, f32[64,512]{1,0:T(8,128)S(1)}) custom-call(bf16[1536,2048]{1,0:T(8,128)(2,1)S(1)} %copy-done.2, bf16[2048,512]{1,0:T(8,128)(2,1)S(1)} %copy-done.6, bf16[64,1536]{1,0:T(8,128)(2,1)S(1)} %bitcast.25, f32[1536,2,1024]{2,1,0:T(2,128)} %master_ref.7, ...), custom_call_target="tpu_custom_call" | custom-call | flops 3221225472 | bytes 25165824 | tf_op jit(solution)/shard_map/pallas_call | solution.py:54
  154.5 20.9 %all-gather.13.cloned.1.call-done.cot_ref = bf16[2048,512]{1,0:T(8,128)(2,1)} async-done(((bf16[512,512]{1,0:T(8,128)(2,1)}), bf16[2048,512]{1,0:T(8,128)(2,1)}) %all-gather.13.cloned.1.call-update) | async-done | bytes 2097168 | tf_op jit(solution)/shard_map/all_gather | solution.py:109
  175.3 2.8 copy-done.3
  178.1 1.6 copy-done.9
  179.7 20.9 %shard_map.103 = (f32[1536,2,1024]{2,1,0:T(2,128)}, f32[1536,2,1024]{2,1,0:T(2,128)}, f32[1536,2,1024]{2,1,0:T(2,128)}, f32[64,512]{1,0:T(8,128)S(1)}) custom-call(bf16[1536,2048]{1,0:T(8,128)(2,1)S(1)} %copy-done.3, bf16[2048,512]{1,0:T(8,128)(2,1)S(1)} %copy-done.9, ...), custom_call_target="tpu_custom_call", output_to_operand_aliasing={{0}: (6, {}), {1}: (7, {}), {2}: (8, {})} | custom-call | flops 3221225472 | bytes 25165824 | tf_op jit(solution)/shard_map/pallas_call | solution.py:54
  200.6 20.8 %all-gather.11.cloned.1.call-done.cot_ref = bf16[2048,512]{1,0:T(8,128)(2,1)} async-done(((bf16[512,512]{1,0:T(8,128)(2,1)}), bf16[2048,512]{1,0:T(8,128)(2,1)}) %all-gather.11.cloned.1.call-update) | async-done | bytes 2097168 | tf_op jit(solution)/shard_map/all_gather | solution.py:109
  221.4 2.8 copy-done.4
  224.2 1.6 copy-done.7
  225.8 20.9 %shard_map.104 = (f32[1536,2,1024]{2,1,0:T(2,128)}, f32[1536,2,1024]{2,1,0:T(2,128)}, f32[1536,2,1024]{2,1,0:T(2,128)}, f32[64,512]{1,0:T(8,128)S(1)}) custom-call(bf16[1536,2048]{1,0:T(8,128)(2,1)S(1)} %copy-done.4, bf16[2048,512]{1,0:T(8,128)(2,1)S(1)} %copy-done.7, ...), custom_call_target="tpu_custom_call", output_to_operand_aliasing={{0}: (6, {}), {1}: (7, {}), {2}: (8, {})} | custom-call | flops 3221225472 | bytes 25165824 | tf_op jit(solution)/shard_map/pallas_call | solution.py:54
  246.7 20.8 %all-gather.9.cloned.1.call-done.cot_ref = bf16[2048,512]{1,0:T(8,128)(2,1)} async-done(((bf16[512,512]{1,0:T(8,128)(2,1)}), bf16[2048,512]{1,0:T(8,128)(2,1)}) %all-gather.9.cloned.1.call-update) | async-done | bytes 2097168 | tf_op jit(solution)/shard_map/all_gather | solution.py:109
  267.5 2.8 copy-done.5
  270.3 1.6 copy-done.8
  271.9 20.9 %shard_map.105 = (f32[1536,2,1024]{2,1,0:T(2,128)}, f32[1536,2,1024]{2,1,0:T(2,128)}, f32[1536,2,1024]{2,1,0:T(2,128)}, f32[64,512]{1,0:T(8,128)S(1)}) custom-call(bf16[1536,2048]{1,0:T(8,128)(2,1)S(1)} %copy-done.5, bf16[2048,512]{1,0:T(8,128)(2,1)S(1)} %copy-done.8, ...), custom_call_target="tpu_custom_call", output_to_operand_aliasing={{0}: (6, {}), {1}: (7, {}), {2}: (8, {})} | custom-call | flops 3221225472 | bytes 25165824 | tf_op jit(solution)/shard_map/pallas_call | solution.py:54
  292.9 0.8 pad_maximum_fusion
  293.7 0.0 reduce-scatter.2.cloned.1.call-update
  293.7 20.5 %reduce-scatter.2.cloned.1.call-done = f32[16,2048]{1,0:T(8,128)} async-done(((f32[64,2048]{1,0:T(8,128)}), f32[16,2048]{1,0:T(8,128)}) %reduce-scatter.2.cloned.1.call-update) | async-done | bytes 131088 | tf_op jit(solution)/shard_map/reduce_scatter | solution.py:114
  314.2 1.0 reshape.70
  315.3 0.4 slice_reduce_fusion.1
  315.7 0.6 multiply_convert_fusion
  (19 shorter events, 0.1 us)
Async XLA Ops:
  7.2 34.9 %copy-start = (bf16[8,6144]{1,0:T(8,128)(2,1)S(1)}, bf16[8,6144]{1,0:T(8,128)(2,1)}, u32[]{:S(2)}) copy-start(bf16[8,6144]{1,0:T(8,128)(2,1)} %param.7) | copy-start | bytes 294916
  7.2 34.9 %copy-start.10 = (s32[8]{0:T(128)S(1)}, s32[8]{0:T(128)}, u32[]{:S(2)}) copy-start(s32[8]{0:T(128)} %param.8) | copy-start | bytes 100
  7.2 73.8 %all-gather.7.cloned.1.call-start = ((), (), s32[]{:S(2)}) async-start(), calls=%async_computation.3 | async-start | bytes 7077888 | tf_op jit(solution)/shard_map/all_gather | solution.py:100
  35.5 93.6 %all-gather.15.cloned.1.call-start = ((), (), s32[]{:S(2)}) async-start(), calls=%async_computation.7 | async-start | bytes 2621440 | tf_op jit(solution)/shard_map/all_gather | solution.py:109
  39.1 136.2 %all-gather.13.cloned.1.call-start = ((), (), s32[]{:S(2)}) async-start(), calls=%async_computation.6 | async-start | bytes 2621440 | tf_op jit(solution)/shard_map/all_gather | solution.py:109
  40.1 181.3 %all-gather.11.cloned.1.call-start = ((), (), s32[]{:S(2)}) async-start(), calls=%async_computation.5 | async-start | bytes 2621440 | tf_op jit(solution)/shard_map/all_gather | solution.py:109
  41.1 226.4 %all-gather.9.cloned.1.call-start = ((), (), s32[]{:S(2)}) async-start(), calls=%async_computation.4 | async-start | bytes 2621440 | tf_op jit(solution)/shard_map/all_gather | solution.py:109
  53.2 42.7 %all-to-all-start.1 = ((bf16[16,4,1536]{2,0,1:T(8,128)(2,1)}), bf16[16,4,1536]{2,0,1:T(8,128)(2,1)S(1)}, u32[]{:S(2)}, u32[]{:S(2)}) async-start(bf16[16,4,1536]{2,0,1:T(8,128)(2,1)} %copy.36), calls=%async_computation.1 | async-start | bytes 393216 | tf_op jit(solution)/shard_map/all_to_all | solution.py:95
  56.5 257.7 %reduce-scatter.2.cloned.1.call-start = ((), (), s32[]{:S(2)}) async-start(), calls=%async_computation.8 | async-start | bytes 655360 | tf_op jit(solution)/shard_map/reduce_scatter | solution.py:114
  129.1 2.8 copy-start.2
  131.8 1.6 copy-start.6
  175.3 2.8 copy-start.3
  178.1 1.6 copy-start.9
  221.4 2.8 copy-start.4
  224.2 1.6 copy-start.7
  267.5 2.8 copy-start.5
  270.3 1.6 copy-start.8
  271.9 44.4 %copy-start.1 = (bf16[8,6144]{1,0:T(8,128)(2,1)S(1)}, bf16[8,6144]{1,0:T(8,128)(2,1)}, u32[]{:S(2)}) copy-start(bf16[8,6144]{1,0:T(8,128)(2,1)} %param.7) | copy-start | bytes 294916
Sparse Core Ops, SparseCore 0:
  35.6 45.2 all-gather.6
  83.1 45.9 all-gather.14
  130.6 44.6 all-gather.12
  176.7 44.6 all-gather.10
  222.9 44.6 all-gather.8
  293.9 20.3 reduce-scatter.1

commit v2 on v1

--- a/solution.py
+++ b/solution.py
@@ -94,29 +94,40 @@
     routed = lax.all_gather(chosen, "exp", axis=0, tiled=True)
     pieces = lax.all_to_all(routed, "rep", split_axis=1, concat_axis=0, tiled=True)
 
+    width = max(128, hidden_dev // 4)
+    chunks = hidden_dev // width
+    sent = [
+        cotangents[0, :, :, chunk * width : (chunk + 1) * width].reshape(saved, 2 * width)
+        for chunk in range(chunks)
+    ]
     part = saved // peers
     own = lax.dynamic_slice_in_dim(rows_in, lax.axis_index("exp") * part, part, 0)
+    cots = [lax.all_gather(sent[0], "rep", axis=0, tiled=True)]
+    own, sent[0] = lax.optimization_barrier((own, sent[0]))
     own = lax.all_to_all(own, "rep", split_axis=1, concat_axis=0, tiled=True)
+    own, cots[0] = lax.optimization_barrier((own, cots[0]))
     everyone = lax.all_gather(own, "exp", axis=0, tiled=True)
+    for chunk in range(1, chunks):
+        sent[chunk], own = lax.optimization_barrier((sent[chunk], own))
+        cots.append(lax.all_gather(sent[chunk], "rep", axis=0, tiled=True))
     everyone = everyone.reshape(peers, replicas, part, row_share)
     rows_t = everyone.transpose(3, 1, 0, 2).reshape(row_share, replicas * saved)
 
-    width = max(128, hidden_dev // 4)
     outs = ()
-    partials = []
-    for chunk in range(hidden_dev // width):
-        piece = cotangents[0, :, :, chunk * width : (chunk + 1) * width].reshape(saved, 2 * width)
-        cot = lax.all_gather(piece, "rep", axis=0, tiled=True)
+    hidden = []
+    own_rows = routed.shape[0]
+    for chunk in range(chunks):
         *outs, pre = adam_chunk(
-            chunk, width, replicas, rows_t, cot, pieces, master, moment1, moment2, tuple(outs)
+            chunk, width, replicas, rows_t, cots[chunk], pieces, master, moment1, moment2, tuple(outs)
         )
-        partials.append(pre)
-    preact = lax.psum_scatter(
-        jnp.concatenate(partials, axis=1), "rep", scatter_dimension=0, tiled=True
-    )
-    preact = preact.reshape(routed.shape[0], hidden_dev // width, 2, width)
-    hidden = (jax.nn.silu(preact[:, :, 0]) * preact[:, :, 1]).astype(jnp.bfloat16)
-    return (*outs, hidden.reshape(1, routed.shape[0], hidden_dev))
+        terms = lax.all_to_all(
+            pre.reshape(replicas, own_rows, 2 * width), "rep", split_axis=0, concat_axis=0, tiled=True
+        )
+        if chunk + 1 < chunks:
+            terms, cots[chunk + 1] = lax.optimization_barrier((terms, cots[chunk + 1]))
+        preact = jnp.sum(terms, axis=0)
+        hidden.append((jax.nn.silu(preact[:, :width]) * preact[:, width:]).astype(jnp.bfloat16))
+    return (*outs, jnp.concatenate(hidden, axis=1)[None])
 
 
 def solution(mesh):

time: 324 us -> 308 us (0.951)
  waiting for transfers between devices: 141 us -> 95.2 us
  blocking collectives: 36.2 us -> 54.8 us
  starting transfers between devices: 3.61 us -> 18.4 us
  local copies, waits for them, and re-layouts: 42.9 us -> 39.4 us
    all_gather x4, waiting for transfers between devices: 95.7 us -> 57.2 us  [the longest x3 41.9 us: shards(): cots.append(lax.all_gather(sent[chunk], 'rep', axis=0, tiled=True))]
    reduce_scatter x1 -> x0, waiting for transfers between devices: 20.5 us -> none  [shards(): lax.psum_scatter(jnp.concatenate(partials, axis=1), 'rep', scatter_dimens...]
    all_to_all x1, blocking collectives: 26.3 us -> 45.1 us  [shards(): own = lax.all_to_all(own, 'rep', split_axis=1, concat_axis=0, tiled=True)]
    all_to_all x0 -> x4, starting transfers between devices: none -> 14.8 us  [shards(): lax.all_to_all(pre.reshape(replicas, own_rows, 2 * width), 'rep', split_a...]
    all_to_all x0 -> x4, waiting for transfers between devices: none -> 8.42 us  [shards(): lax.all_to_all(pre.reshape(replicas, own_rows, 2 * width), 'rep', split_a...]
    all_gather x1, waiting for transfers between devices: 24.4 us -> 29.5 us  [shards(): everyone = lax.all_gather(own, 'exp', axis=0, tiled=True)]
  transfers between devices with their start and end apart: 7 -> 10, of which waited for: 6 -> 7; matrix products, arithmetic and copies ran while one was open for 7% -> 7% of each run, Pallas kernels for 19% -> 21%
where the time goes in v2:
time: 308 us; the launch traced here: 307 us
  waiting for transfers between devices  95.2 us (31%)
  Pallas kernels  84.4 us (27%)
  blocking collectives  54.8 us (18%)
  local copies, waits for them, and re-layouts  39.4 us (13%)
  starting transfers between devices  18.4 us (6%)
  between operations  14 us (5%)
    pallas_call x4, Pallas kernels, adam_chunk(): pl.pallas_call(functools.partial(adam_kernel, replicas, passed), grid=(sh...  84.4 us
    all_to_all x1, blocking collectives, shards(): own = lax.all_to_all(own, 'rep', split_axis=1, concat_axis=0, tiled=True)  45.1 us
    all_gather x3, waiting for transfers between devices, shards(): cots.append(lax.all_gather(sent[chunk], 'rep', axis=0, tiled=True))  41.9 us
    all_gather x1, waiting for transfers between devices, shards(): everyone = lax.all_gather(own, 'exp', axis=0, tiled=True)  29.5 us
    unnamed x26, local copies, waits for them, and re-layouts  19.5 us
    all_gather x1, waiting for transfers between devices, shards(): cots = [lax.all_gather(sent[0], 'rep', axis=0, tiled=True)]  15.2 us
    all_to_all x4, starting transfers between devices, shards(): lax.all_to_all(pre.reshape(replicas, own_rows, 2 * width), 'rep', split_a...  14.8 us
    all_gather x1, blocking collectives, shards(): routed = lax.all_gather(chosen, 'exp', axis=0, tiled=True)  9.65 us
  transfers between devices with their start and end apart: 10, of which 7 were waited for; matrix products, arithmetic and copies ran while one was open for 7% of the time, Pallas kernels for 21%

profile of v2, /device:TPU:0, one launch (start us, length us, event | category | flops | bytes accessed | tf_op | source)
XLA Modules:
  0.0 307.1 jit_solution(16348029414304045110)
XLA Ops:
  7.2 0.0 all-gather.7.cloned.1.call-start
  7.2 2.7 fusion.6
  9.9 0.9 copy.42
  10.8 0.0 all-gather.7.cloned.1.call-update
  10.8 0.0 all-gather.9.cloned.1.call-start
  10.9 1.2 dynamic-slice_bitcast_fusion
  12.1 0.1 copy.47
  12.1 45.1 %all_to_all.58 = bf16[64,4,1536]{2,0,1:T(8,128)(2,1)} all-to-all(bf16[64,4,1536]{2,0,1:T(8,128)(2,1)S(1)} %bitcast.45), channel_id=1, replica_groups=mesh['exp'=8,'rep'=4] {'rep'}, dimensions={1} | all-to-all | bytes 1572864 | tf_op jit(solution)/shard_map/all_to_all | solution.py:107
  57.3 15.2 %all-gather.7.cloned.1.call-done.cot_ref = bf16[2048,512]{1,0:T(8,128)(2,1)} async-done(((bf16[512,512]{1,0:T(8,128)(2,1)}), bf16[2048,512]{1,0:T(8,128)(2,1)}) %all-gather.7.cloned.1.call-update) | async-done | bytes 2097168 | tf_op jit(solution)/shard_map/all_gather | solution.py:105
  72.5 0.0 all-gather.9.cloned.1.call-update
  72.5 0.0 all-gather.11.cloned.1.call-start
  72.6 0.9 copy.43
  73.5 0.0 all-gather.11.cloned.1.call-update
  73.5 0.0 all-gather.13.cloned.1.call-start
  73.5 0.9 copy.44
  74.4 0.0 all-gather.13.cloned.1.call-update
  74.5 0.0 all-gather.15.cloned.1.call-start
  74.5 0.9 copy.45
  75.4 0.0 all-gather.15.cloned.1.call-update
  75.5 0.3 fusion
  75.8 9.7 %all-gather = bf16[8,2,6144]{2,1,0:T(2,128)(2,1)S(1)} all-gather(bf16[1,2,6144]{2,1,0:T(2,128)(2,1)S(1)} %fusion), channel_id=1, replica_groups=mesh['exp'=8,'rep'=4] {'exp'}, dimensions={0}, use_global_device_ids=true | all-gather | bytes 221184 | tf_op jit(solution)/shard_map/all_gather | solution.py:94
  85.4 0.1 all_to_all.44
  85.6 0.7 copy.36
  86.3 3.4 %all-to-all-start.1 = ((bf16[16,4,1536]{2,0,1:T(8,128)(2,1)}), bf16[16,4,1536]{2,0,1:T(8,128)(2,1)S(1)}, u32[]{:S(2)}, u32[]{:S(2)}) async-start(bf16[16,4,1536]{2,0,1:T(8,128)(2,1)} %copy.36), calls=%async_computation.1 | async-start | bytes 393216 | tf_op jit(solution)/shard_map/all_to_all | solution.py:95
  89.6 29.5 %all-gather.9.cloned.1.call-done = bf16[2048,1536]{1,0:T(8,128)(2,1)} async-done(((bf16[256,1536]{1,0:T(8,128)(2,1)}), bf16[2048,1536]{1,0:T(8,128)(2,1)}) %all-gather.9.cloned.1.call-update) | async-done | bytes 6291472 | tf_op jit(solution)/shard_map/all_gather | solution.py:109
  119.2 6.3 %copy.35 = bf16[1536,4,8,64]{0,3,2,1:T(8,128)(2,1)} copy(bf16[1536,4,8,64]{0,3,1,2:T(8,128)(2,1)} %bitcast.42) | data formatting | bytes 12582912 | tf_op jit(solution)/shard_map/transpose | solution.py:114
  125.5 8.8 %copy.40.rows_ref = bf16[1536,2048]{1,0:T(8,128)(2,1)} copy(bf16[1536,2048]{0,1:T(8,128)(2,1)} %bitcast.41) | data formatting | bytes 12582912 | tf_op jit(solution)/shard_map/reshape | solution.py:114
  134.2 2.8 copy-done.2
  137.0 21.1 %shard_map.102 = (f32[1536,2,1024]{2,1,0:T(2,128)}, f32[1536,2,1024]{2,1,0:T(2,128)}, f32[1536,2,1024]{2,1,0:T(2,128)}, f32[64,512]{1,0:T(8,128)}) custom-call(bf16[1536,2048]{1,0:T(8,128)(2,1)S(1)} %copy-done.2, bf16[2048,512]{1,0:T(8,128)(2,1)S(1)} %copy-done.6, bf16[64,1536]{1,0:T(8,128)(2,1)S(1)} %bitcast.37, f32[1536,2,1024]{2,1,0:T(2,128)} %master_ref.7, ...), custom_call_target="tpu_custom_call" | custom-call | flops 3221225472 | bytes 25165824 | tf_op jit(solution)/shard_map/pallas_call | solution.py:54
  158.1 4.6 %all-to-all-start.2 = ((f32[4,16,512]{2,1,0:T(8,128)}), f32[4,16,512]{2,1,0:T(8,128)S(1)}, u32[]{:S(2)}, u32[]{:S(2)}) async-start(f32[4,16,512]{2,1,0:T(8,128)} %bitcast.9), calls=%async_computation.2 | async-start | bytes 262144 | tf_op jit(solution)/shard_map/all_to_all | solution.py:123
  162.7 4.1 %all-gather.11.cloned.1.call-done.cot_ref = bf16[2048,512]{1,0:T(8,128)(2,1)} async-done(((bf16[512,512]{1,0:T(8,128)(2,1)}), bf16[2048,512]{1,0:T(8,128)(2,1)}) %all-gather.11.cloned.1.call-update) | async-done | bytes 2097168 | tf_op jit(solution)/shard_map/all_gather | solution.py:112
  166.8 2.3 all-to-all-done.2
  169.1 2.8 copy-done.3
  171.9 1.6 copy-done.9
  173.5 21.2 %shard_map.103 = (f32[1536,2,1024]{2,1,0:T(2,128)}, f32[1536,2,1024]{2,1,0:T(2,128)}, f32[1536,2,1024]{2,1,0:T(2,128)}, f32[64,512]{1,0:T(8,128)}) custom-call(bf16[1536,2048]{1,0:T(8,128)(2,1)S(1)} %copy-done.3, bf16[2048,512]{1,0:T(8,128)(2,1)S(1)} %copy-done.9, ...), custom_call_target="tpu_custom_call", output_to_operand_aliasing={{0}: (6, {}), {1}: (7, {}), {2}: (8, {})} | custom-call | flops 3221225472 | bytes 25165824 | tf_op jit(solution)/shard_map/pallas_call | solution.py:54
  194.7 3.3 %all-to-all-start.3 = ((f32[4,16,512]{2,1,0:T(8,128)}), f32[4,16,512]{2,1,0:T(8,128)S(1)}, u32[]{:S(2)}, u32[]{:S(2)}) async-start(f32[4,16,512]{2,1,0:T(8,128)} %bitcast.10), calls=%async_computation.3 | async-start | bytes 262144 | tf_op jit(solution)/shard_map/all_to_all | solution.py:123
  198.0 18.0 %all-gather.13.cloned.1.call-done.cot_ref = bf16[2048,512]{1,0:T(8,128)(2,1)} async-done(((bf16[512,512]{1,0:T(8,128)(2,1)}), bf16[2048,512]{1,0:T(8,128)(2,1)}) %all-gather.13.cloned.1.call-update) | async-done | bytes 2097168 | tf_op jit(solution)/shard_map/all_gather | solution.py:112
  216.0 2.8 copy-done.4
  218.8 1.6 copy-done.8
  220.4 21.1 %shard_map.104 = (f32[1536,2,1024]{2,1,0:T(2,128)}, f32[1536,2,1024]{2,1,0:T(2,128)}, f32[1536,2,1024]{2,1,0:T(2,128)}, f32[64,512]{1,0:T(8,128)}) custom-call(bf16[1536,2048]{1,0:T(8,128)(2,1)S(1)} %copy-done.4, bf16[2048,512]{1,0:T(8,128)(2,1)S(1)} %copy-done.8, ...), custom_call_target="tpu_custom_call", output_to_operand_aliasing={{0}: (6, {}), {1}: (7, {}), {2}: (8, {})} | custom-call | flops 3221225472 | bytes 25165824 | tf_op jit(solution)/shard_map/pallas_call | solution.py:54
  241.5 3.5 %all-to-all-start.4 = ((f32[4,16,512]{2,1,0:T(8,128)}), f32[4,16,512]{2,1,0:T(8,128)S(1)}, u32[]{:S(2)}, u32[]{:S(2)}) async-start(f32[4,16,512]{2,1,0:T(8,128)} %bitcast.11), calls=%async_computation.4 | async-start | bytes 262144 | tf_op jit(solution)/shard_map/all_to_all | solution.py:123
  245.1 19.9 %all-gather.15.cloned.1.call-done.cot_ref = bf16[2048,512]{1,0:T(8,128)(2,1)} async-done(((bf16[512,512]{1,0:T(8,128)(2,1)}), bf16[2048,512]{1,0:T(8,128)(2,1)}) %all-gather.15.cloned.1.call-update) | async-done | bytes 2097168 | tf_op jit(solution)/shard_map/all_gather | solution.py:112
  264.9 2.8 copy-done.5
  267.7 1.6 copy-done.7
  269.3 21.1 %shard_map.105 = (f32[1536,2,1024]{2,1,0:T(2,128)}, f32[1536,2,1024]{2,1,0:T(2,128)}, f32[1536,2,1024]{2,1,0:T(2,128)}, f32[64,512]{1,0:T(8,128)}) custom-call(bf16[1536,2048]{1,0:T(8,128)(2,1)S(1)} %copy-done.5, bf16[2048,512]{1,0:T(8,128)(2,1)S(1)} %copy-done.7, ...), custom_call_target="tpu_custom_call", output_to_operand_aliasing={{0}: (6, {}), {1}: (7, {}), {2}: (8, {})} | custom-call | flops 3221225472 | bytes 25165824 | tf_op jit(solution)/shard_map/pallas_call | solution.py:54
  290.4 3.3 %all-to-all-start.5 = ((f32[4,16,512]{2,1,0:T(8,128)}), f32[4,16,512]{2,1,0:T(8,128)S(1)}, u32[]{:S(2)}, u32[]{:S(2)}) async-start(f32[4,16,512]{2,1,0:T(8,128)} %bitcast.12), calls=%async_computation.5 | async-start | bytes 262144 | tf_op jit(solution)/shard_map/all_to_all | solution.py:123
  293.8 6.1 %all-to-all-done.5 = f32[4,16,512]{2,1,0:T(8,128)S(1)} async-done(((f32[4,16,512]{2,1,0:T(8,128)}), f32[4,16,512]{2,1,0:T(8,128)S(1)}, u32[]{:S(2)}, u32[]{:S(2)}) %all-to-all-start.5) | async-done | bytes 131104 | tf_op jit(solution)/shard_map/all_to_all | solution.py:123
  300.0 0.6 maximum_bitcast_fusion
  (25 shorter events, 0.1 us)
Async XLA Ops:
  7.2 68.3 %copy-start = (bf16[8,6144]{1,0:T(8,128)(2,1)S(1)}, bf16[8,6144]{1,0:T(8,128)(2,1)}, u32[]{:S(2)}) copy-start(bf16[8,6144]{1,0:T(8,128)(2,1)} %param.7) | copy-start | bytes 294916
  7.2 68.3 %copy-start.10 = (s32[8]{0:T(128)S(1)}, s32[8]{0:T(128)}, u32[]{:S(2)}) copy-start(s32[8]{0:T(128)} %param.8) | copy-start | bytes 100
  7.2 65.3 %all-gather.7.cloned.1.call-start = ((), (), s32[]{:S(2)}) async-start(), calls=%async_computation.6 | async-start | bytes 2621440 | tf_op jit(solution)/shard_map/all_gather | solution.py:105
  10.8 108.3 %all-gather.9.cloned.1.call-start = ((), (), s32[]{:S(2)}) async-start(), calls=%async_computation.7 | async-start | bytes 7077888 | tf_op jit(solution)/shard_map/all_gather | solution.py:109
  72.5 94.3 %all-gather.11.cloned.1.call-start = ((), (), s32[]{:S(2)}) async-start(), calls=%async_computation.8 | async-start | bytes 2621440 | tf_op jit(solution)/shard_map/all_gather | solution.py:112
  73.5 142.5 %all-gather.13.cloned.1.call-start = ((), (), s32[]{:S(2)}) async-start(), calls=%async_computation.9 | async-start | bytes 2621440 | tf_op jit(solution)/shard_map/all_gather | solution.py:112
  74.5 190.4 %all-gather.15.cloned.1.call-start = ((), (), s32[]{:S(2)}) async-start(), calls=%async_computation.10 | async-start | bytes 2621440 | tf_op jit(solution)/shard_map/all_gather | solution.py:112
  86.3 48.0 %all-to-all-start.1 = ((bf16[16,4,1536]{2,0,1:T(8,128)(2,1)}), bf16[16,4,1536]{2,0,1:T(8,128)(2,1)S(1)}, u32[]{:S(2)}, u32[]{:S(2)}) async-start(bf16[16,4,1536]{2,0,1:T(8,128)(2,1)} %copy.36), calls=%async_computation.1 | async-start | bytes 393216 | tf_op jit(solution)/shard_map/all_to_all | solution.py:95
  119.2 15.1 %copy-start.6 = (bf16[2048,512]{1,0:T(8,128)(2,1)S(1)}, bf16[2048,512]{1,0:T(8,128)(2,1)}, u32[]{:S(2)}) copy-start(bf16[2048,512]{1,0:T(8,128)(2,1)} %all-gather.7.cloned.1.call-done.cot_ref) | copy-start | bytes 6291460
  134.2 2.8 copy-start.2
  158.1 11.0 %all-to-all-start.2 = ((f32[4,16,512]{2,1,0:T(8,128)}), f32[4,16,512]{2,1,0:T(8,128)S(1)}, u32[]{:S(2)}, u32[]{:S(2)}) async-start(f32[4,16,512]{2,1,0:T(8,128)} %bitcast.9), calls=%async_computation.2 | async-start | bytes 262144 | tf_op jit(solution)/shard_map/all_to_all | solution.py:123
  169.1 2.8 copy-start.3
  171.9 1.6 copy-start.9
  194.7 21.4 %all-to-all-start.3 = ((f32[4,16,512]{2,1,0:T(8,128)}), f32[4,16,512]{2,1,0:T(8,128)S(1)}, u32[]{:S(2)}, u32[]{:S(2)}) async-start(f32[4,16,512]{2,1,0:T(8,128)} %bitcast.10), calls=%async_computation.3 | async-start | bytes 262144 | tf_op jit(solution)/shard_map/all_to_all | solution.py:123
  216.0 2.8 copy-start.4
  218.8 1.6 copy-start.8
  241.5 23.4 %all-to-all-start.4 = ((f32[4,16,512]{2,1,0:T(8,128)}), f32[4,16,512]{2,1,0:T(8,128)S(1)}, u32[]{:S(2)}, u32[]{:S(2)}) async-start(f32[4,16,512]{2,1,0:T(8,128)} %bitcast.11), calls=%async_computation.4 | async-start | bytes 262144 | tf_op jit(solution)/shard_map/all_to_all | solution.py:123
  264.9 2.8 copy-start.5
  267.7 1.6 copy-start.7
  269.3 31.3 %copy-start.1 = (bf16[8,6144]{1,0:T(8,128)(2,1)S(1)}, bf16[8,6144]{1,0:T(8,128)(2,1)}, u32[]{:S(2)}) copy-start(bf16[8,6144]{1,0:T(8,128)(2,1)} %param.7) | copy-start | bytes 294916
  290.4 9.5 %all-to-all-start.5 = ((f32[4,16,512]{2,1,0:T(8,128)}), f32[4,16,512]{2,1,0:T(8,128)S(1)}, u32[]{:S(2)}, u32[]{:S(2)}) async-start(f32[4,16,512]{2,1,0:T(8,128)} %bitcast.12), calls=%async_computation.5 | async-start | bytes 262144 | tf_op jit(solution)/shard_map/all_to_all | solution.py:123
Sparse Core Ops, SparseCore 0:
  10.9 61.5 all-gather.6
  74.4 44.7 all-gather.8
  120.7 46.0 all-gather.10
  168.2 47.7 all-gather.12
  217.4 47.4 all-gather.14

commit v3 on v2

--- a/solution.py
+++ b/solution.py
@@ -30,10 +30,10 @@
     for g in range(2):
         cols = slice(g * width, (g + 1) * width)
         total = jnp.dot(rows_ref[...], cot_ref[:, cols], preferred_element_type=jnp.float32)
-        average = total / replicas
+        average = total * (1.0 / replicas)
         new_first = 0.9 * first_ref[:, g, :] + 0.1 * average
         new_second = 0.999 * second_ref[:, g, :] + 0.001 * average * average
-        ratio = new_first / correct_one / (jnp.sqrt(new_second / correct_two) + 1e-08)
+        ratio = new_first * (1.0 / correct_one) / (jnp.sqrt(new_second * (1.0 / correct_two)) + 1e-08)
         old = master_ref[:, g, :]
         new_master = old - 0.001 * (ratio + 0.1 * old)
         out_first[:, g, :] = new_first
@@ -71,8 +71,38 @@
             bytes_accessed=24 * share * 2 * width + 2 * share * depth,
             transcendentals=0,
         ),
-        compiler_params=pltpu.CompilerParams(vmem_limit_bytes=40 * 1024 * 1024),
+        compiler_params=pltpu.CompilerParams(vmem_limit_bytes=56 * 1024 * 1024),
     )(rows_t, cot, pieces, master, first, second, *before)
+
+
+def gather_rows(own, peers):
+    replicas = lax.axis_size("rep")
+    part, row_share = own.shape[0] // replicas, own.shape[1]
+    bits = peers.bit_length() - 1
+    if bits < 2 or peers != 1 << bits or row_share % 2:
+        return lax.all_gather(own, "exp", axis=0).reshape(peers, replicas, part, row_share)
+    me = lax.axis_index("exp")
+    upper = list(range(1, bits))
+    half = row_share // 2
+    chains = [
+        own[:, h * half : (h + 1) * half].reshape((1,) * bits + (replicas, part, half))
+        for h in range(2)
+    ]
+    orders = [upper + [0], upper[::-1] + [0]]
+    for step in range(bits):
+        arrived = [
+            lax.ppermute(chain, "exp", [(i, i ^ (1 << order[step])) for i in range(peers)])
+            for chain, order in zip(chains, orders)
+        ]
+        for h in range(2):
+            bit = orders[h][step]
+            odd = (me >> bit) % 2 == 1
+            low = jnp.where(odd, arrived[h], chains[h])
+            high = jnp.where(odd, chains[h], arrived[h])
+            chains[h] = jnp.concatenate([low, high], axis=bits - 1 - bit)
+    return jnp.concatenate(
+        [chain.reshape(peers, replicas, part, half) for chain in chains], axis=3
+    )
 
 
 def shards(tokens, slot_index, saved_inputs, cotangents, master, moment1, moment2):
@@ -94,11 +124,15 @@
     routed = lax.all_gather(chosen, "exp", axis=0, tiled=True)
     pieces = lax.all_to_all(routed, "rep", split_axis=1, concat_axis=0, tiled=True)
 
-    width = max(128, hidden_dev // 4)
-    chunks = hidden_dev // width
+    if hidden_dev % 1024 == 0:
+        unit = hidden_dev // 8
+        spans = [(0, 2 * unit), (3 * unit, 3 * unit), (6 * unit, 2 * unit), (2 * unit, unit)]
+    else:
+        spans = [(0, hidden_dev)]
+    chunks = len(spans)
     sent = [
-        cotangents[0, :, :, chunk * width : (chunk + 1) * width].reshape(saved, 2 * width)
-        for chunk in range(chunks)
+        cotangents[0, :, :, start : start + width].reshape(saved, 2 * width)
+        for start, width in spans
     ]
     part = saved // peers
     own = lax.dynamic_slice_in_dim(rows_in, lax.axis_index("exp") * part, part, 0)
@@ -106,19 +140,19 @@
     own, sent[0] = lax.optimization_barrier((own, sent[0]))
     own = lax.all_to_all(own, "rep", split_axis=1, concat_axis=0, tiled=True)
     own, cots[0] = lax.optimization_barrier((own, cots[0]))
-    everyone = lax.all_gather(own, "exp", axis=0, tiled=True)
+    everyone = gather_rows(own, peers)
     for chunk in range(1, chunks):
         sent[chunk], own = lax.optimization_barrier((sent[chunk], own))
         cots.append(lax.all_gather(sent[chunk], "rep", axis=0, tiled=True))
-    everyone = everyone.reshape(peers, replicas, part, row_share)
     rows_t = everyone.transpose(3, 1, 0, 2).reshape(row_share, replicas * saved)
 
     outs = ()
     hidden = []
     own_rows = routed.shape[0]
     for chunk in range(chunks):
+        start, width = spans[chunk]
         *outs, pre = adam_chunk(
-            chunk, width, replicas, rows_t, cots[chunk], pieces, master, moment1, moment2, tuple(outs)
+            start // width, width, replicas, rows_t, cots[chunk], pieces, master, moment1, moment2, tuple(outs)
         )
         terms = lax.all_to_all(
             pre.reshape(replicas, own_rows, 2 * width), "rep", split_axis=0, concat_axis=0, tiled=True
@@ -127,6 +161,7 @@
             terms, cots[chunk + 1] = lax.optimization_barrier((terms, cots[chunk + 1]))
         preact = jnp.sum(terms, axis=0)
         hidden.append((jax.nn.silu(preact[:, :width]) * preact[:, width:]).astype(jnp.bfloat16))
+    hidden = [block for _, block in sorted(zip([start for start, _ in spans], hidden), key=lambda pair: pair[0])]
     return (*outs, jnp.concatenate(hidden, axis=1)[None])
 
 

time: 308 us -> 287 us (0.932)
  blocking collectives: 54.8 us -> 24.2 us
  local copies, waits for them, and re-layouts: 39.4 us -> 24.1 us
  starting transfers between devices: 18.4 us -> 27.3 us
  other arithmetic: 0.72 us -> 8.15 us
  waiting for transfers between devices: 95.2 us -> 100 us
  Pallas kernels: 84.4 us -> 87.7 us
    all_gather x3, waiting for transfers between devices: 41.9 us -> 0.04 us  [shards(): cots.append(lax.all_gather(sent[chunk], 'rep', axis=0, tiled=True))]
    all_to_all x0 -> x1, waiting for transfers between devices: none -> 40.4 us  [shards(): own = lax.all_to_all(own, 'rep', split_axis=1, concat_axis=0, tiled=True)]
    all_to_all x1, blocking collectives: 45.1 us -> 15 us  [shards(): lax.all_to_all(pre.reshape(replicas, own_rows, 2 * width), 'rep', split_a...]
    all_gather x1 -> x0, waiting for transfers between devices: 29.5 us -> none  [shards(): everyone = lax.all_gather(own, 'exp', axis=0, tiled=True)]
    ppermute x0 -> x6, waiting for transfers between devices: none -> 22.6 us  [gather_rows(): lax.ppermute(chain, 'exp', [(i, i ^ 1 << order[step]) for i in range(peer...]
    all_to_all x4 -> x3, waiting for transfers between devices: 8.42 us -> 24.2 us  [shards(): lax.all_to_all(pre.reshape(replicas, own_rows, 2 * width), 'rep', split_a...]
    unnamed x26 -> x12, local copies, waits for them, and re-layouts: 19.5 us -> 4.27 us
    ppermute x0 -> x6, starting transfers between devices: none -> 6.72 us  [gather_rows(): lax.ppermute(chain, 'exp', [(i, i ^ 1 << order[step]) for i in range(peer...]
  transfers between devices with their start and end apart: 10 -> 15, of which waited for: 7 -> 7; matrix products, arithmetic and copies ran while one was open for 7% -> 10% of each run, Pallas kernels for 21% -> 25%
where the time goes in v3:
time: 287 us; the launch traced here: 286 us
  waiting for transfers between devices  100 us (35%)
  Pallas kernels  87.7 us (31%)
  starting transfers between devices  27.3 us (10%)
  blocking collectives  24.2 us (8%)
  local copies, waits for them, and re-layouts  24.1 us (8%)
  between operations  14 us (5%)
  other arithmetic  8.15 us (3%)
    pallas_call x4, Pallas kernels, adam_chunk(): pl.pallas_call(functools.partial(adam_kernel, replicas, passed), grid=(sh...  87.7 us
    all_to_all x1, waiting for transfers between devices, shards(): own = lax.all_to_all(own, 'rep', split_axis=1, concat_axis=0, tiled=True)  40.4 us
    all_to_all x3, waiting for transfers between devices, shards(): lax.all_to_all(pre.reshape(replicas, own_rows, 2 * width), 'rep', split_a...  24.2 us
    ppermute x6, waiting for transfers between devices, gather_rows(): lax.ppermute(chain, 'exp', [(i, i ^ 1 << order[step]) for i in range(peer...  22.6 us
    all_to_all x1, blocking collectives, shards(): lax.all_to_all(pre.reshape(replicas, own_rows, 2 * width), 'rep', split_a...  15 us
    all_gather x1, waiting for transfers between devices, shards(): cots = [lax.all_gather(sent[0], 'rep', axis=0, tiled=True)]  13 us
    all_to_all x3, starting transfers between devices, shards(): lax.all_to_all(pre.reshape(replicas, own_rows, 2 * width), 'rep', split_a...  10.7 us
    all_gather x1, blocking collectives, shards(): routed = lax.all_gather(chosen, 'exp', axis=0, tiled=True)  9.28 us
  transfers between devices with their start and end apart: 15, of which 7 were waited for; matrix products, arithmetic and copies ran while one was open for 10% of the time, Pallas kernels for 25%

profile of v3, /device:TPU:0, one launch (start us, length us, event | category | flops | bytes accessed | tf_op | source)
XLA Modules:
  0.0 286.0 jit_solution(16915664005631132433)
XLA Ops:
  7.2 1.9 fusion.6
  9.2 0.9 copy.46
  10.1 1.3 dynamic-slice_bitcast_fusion
  11.3 0.9 copy.52
  12.3 6.3 %all-to-all-start = ((bf16[64,4,1536]{2,0,1:T(8,128)(2,1)}), bf16[64,4,1536]{2,0,1:T(8,128)(2,1)S(1)}, u32[]{:S(2)}, u32[]{:S(2)}) async-start(bf16[64,4,1536]{2,0,1:T(8,128)(2,1)} %bitcast.40), calls=%async_computation | async-start | bytes 1572864 | tf_op jit(solution)/shard_map/all_to_all | solution.py:141
  18.6 1.0 copy.47
  19.6 40.4 %all-to-all-done = bf16[64,4,1536]{2,0,1:T(8,128)(2,1)S(1)} async-done(((bf16[64,4,1536]{2,0,1:T(8,128)(2,1)}), bf16[64,4,1536]{2,0,1:T(8,128)(2,1)S(1)}, u32[]{:S(2)}, u32[]{:S(2)}) %all-to-all-start) | async-done | bytes 786464 | tf_op jit(solution)/shard_map/all_to_all | solution.py:141
  60.0 13.0 %all-gather.6.cloned.1.call-done.cot_ref = bf16[2048,512]{1,0:T(8,128)(2,1)} async-done(((bf16[512,512]{1,0:T(8,128)(2,1)}), bf16[2048,512]{1,0:T(8,128)(2,1)}) %all-gather.6.cloned.1.call-update) | async-done | bytes 2097168 | tf_op jit(solution)/shard_map/all_gather | solution.py:139
  73.1 1.6 collective-permute-start
  74.7 1.5 collective-permute-start.3
  76.2 8.0 %collective-permute-done = bf16[1,1,1,4,64,768]{5,4,3,2,1,0:T(8,128)(2,1)S(1)} collective-permute-done((bf16[1,1,1,4,64,768]{5,4,3,2,1,0:T(8,128)(2,1)S(1)}, bf16[1,1,1,4,64,768]{5,4,3,2,1,0:T(8,128)(2,1)S(1)}, u32[]{:S(2)}, u32[]{:S(2)}) %collective-permute-start) | collective-permute-done | bytes 393248 | tf_op jit(solution)/shard_map/ppermute | solution.py:94
  84.3 0.1 pad_maximum_fusion.5
  84.4 1.6 collective-permute-start.1
  85.9 0.9 copy.48
  87.0 0.1 pad_maximum_fusion.6
  87.1 1.6 collective-permute-start.4
  88.6 14.5 %collective-permute-done.1 = bf16[1,2,1,4,64,768]{5,4,3,2,1,0:T(8,128)(2,1)} collective-permute-done((bf16[1,2,1,4,64,768]{5,4,3,2,1,0:T(8,128)(2,1)S(1)}, bf16[1,2,1,4,64,768]{5,4,3,2,1,0:T(8,128)(2,1)}, u32[]{:S(2)}, u32[]{:S(2)}) %collective-permute-start.1) | collective-permute-done | bytes 786464 | tf_op jit(solution)/shard_map/ppermute | solution.py:94
  103.2 1.2 broadcast_select_fusion.7
  104.4 1.3 pad_maximum_fusion.3
  105.7 0.1 broadcast_select_fusion.5
  105.8 1.3 pad_maximum_fusion.4
  107.1 0.5 collective-permute-start.5
  107.6 0.3 fusion
  107.9 9.3 %all-gather = bf16[8,2,6144]{2,1,0:T(2,128)(2,1)S(1)} all-gather(bf16[1,2,6144]{2,1,0:T(2,128)(2,1)S(1)} %fusion), channel_id=1, replica_groups=mesh['exp'=8,'rep'=4] {'exp'}, dimensions={0}, use_global_device_ids=true | all-gather | bytes 221184 | tf_op jit(solution)/shard_map/all_gather | solution.py:124
  117.2 0.8 all_to_all.44
  118.0 1.6 copy.39
  119.6 3.4 %all-to-all-start.1 = ((bf16[16,4,1536]{2,0,1:T(8,128)(2,1)}), bf16[16,4,1536]{2,0,1:T(8,128)(2,1)S(1)}, u32[]{:S(2)}, u32[]{:S(2)}) async-start(bf16[16,4,1536]{2,0,1:T(8,128)(2,1)} %copy.39), calls=%async_computation.1 | async-start | bytes 393216 | tf_op jit(solution)/shard_map/all_to_all | solution.py:125
  123.0 1.1 slice.47
  124.2 0.8 copy.53
  125.0 2.1 broadcast_select_fusion.1
  127.1 0.3 pad_maximum_fusion.1
  127.4 0.3 pad_maximum_fusion.2
  127.7 0.6 pad_maximum_fusion
  128.2 3.4 %copy.44 = bf16[8,4,64,1536]{3,2,0,1:T(8,128)(2,1)} copy(bf16[8,4,64,1536]{3,2,1,0:T(8,128)(2,1)S(1)} %pad_maximum_fusion) | data formatting | bytes 12582912 | tf_op jit(solution)/shard_map/concatenate | solution.py:103
  131.6 8.7 %copy.43.rows_ref = bf16[1536,2048]{1,0:T(8,128)(2,1)} copy(bf16[1536,2048]{0,1:T(8,128)(2,1)} %bitcast.42) | data formatting | bytes 12582912 | tf_op jit(solution)/shard_map/reshape | solution.py:147
  140.3 0.7 copy-done.2
  141.0 22.2 %shard_map.102 = (f32[1536,2,1024]{2,1,0:T(2,128)}, f32[1536,2,1024]{2,1,0:T(2,128)}, f32[1536,2,1024]{2,1,0:T(2,128)}, f32[64,512]{1,0:T(8,128)}) custom-call(bf16[1536,2048]{1,0:T(8,128)(2,1)} %copy.43.rows_ref, bf16[2048,512]{1,0:T(8,128)(2,1)} %all-gather.6.cloned.1.call-done.cot_ref, bf16[64,1536]{1,0:T(8,128)(2,1)} %bitcast.45, ...), custom_call_target="tpu_custom_call" | custom-call | flops 3221225472 | bytes 25165824 | tf_op jit(solution)/shard_map/pallas_call | solution.py:54
  163.2 15.0 %all_to_all.58 = f32[4,16,512]{2,1,0:T(8,128)S(1)} all-to-all(f32[4,16,512]{2,1,0:T(8,128)} %bitcast.65), channel_id=1, replica_groups=mesh['exp'=8,'rep'=4] {'rep'}, dimensions={0} | all-to-all | bytes 262144 | tf_op jit(solution)/shard_map/all_to_all | solution.py:157
  178.2 27.1 %shard_map.103 = (f32[1536,2,1024]{2,1,0:T(2,128)}, f32[1536,2,1024]{2,1,0:T(2,128)}, f32[1536,2,1024]{2,1,0:T(2,128)}, f32[64,768]{1,0:T(8,128)}) custom-call(bf16[1536,2048]{1,0:T(8,128)(2,1)} %copy.43.rows_ref, bf16[2048,768]{1,0:T(8,128)(2,1)} %all-gather.8.cloned.1.call-done.cot_ref, ...), custom_call_target="tpu_custom_call", output_to_operand_aliasing={{0}: (6, {}), {1}: (7, {}), {2}: (8, {})} | custom-call | flops 4831838208 | bytes 34603008 | tf_op jit(solution)/shard_map/pallas_call | solution.py:54
  205.3 4.1 %all-to-all-start.3 = ((f32[4,16,768]{2,1,0:T(8,128)}), f32[4,16,768]{2,1,0:T(8,128)S(1)}, u32[]{:S(2)}, u32[]{:S(2)}) async-start(f32[4,16,768]{2,1,0:T(8,128)} %bitcast.63), calls=%async_computation.3 | async-start | bytes 393216 | tf_op jit(solution)/shard_map/all_to_all | solution.py:157
  209.5 12.7 %all-to-all-done.3 = f32[4,16,768]{2,1,0:T(8,128)S(1)} async-done(((f32[4,16,768]{2,1,0:T(8,128)}), f32[4,16,768]{2,1,0:T(8,128)S(1)}, u32[]{:S(2)}, u32[]{:S(2)}) %all-to-all-start.3) | async-done | bytes 196640 | tf_op jit(solution)/shard_map/all_to_all | solution.py:157
  222.3 22.4 %shard_map.104 = (f32[1536,2,1024]{2,1,0:T(2,128)}, f32[1536,2,1024]{2,1,0:T(2,128)}, f32[1536,2,1024]{2,1,0:T(2,128)}, f32[64,512]{1,0:T(8,128)}) custom-call(bf16[1536,2048]{1,0:T(8,128)(2,1)} %copy.43.rows_ref, bf16[2048,512]{1,0:T(8,128)(2,1)} %all-gather.10.cloned.1.call-done.cot_ref, ...), custom_call_target="tpu_custom_call", output_to_operand_aliasing={{0}: (6, {}), {1}: (7, {}), {2}: (8, {})} | custom-call | flops 3221225472 | bytes 25165824 | tf_op jit(solution)/shard_map/pallas_call | solution.py:54
  244.6 3.3 %all-to-all-start.4 = ((f32[4,16,512]{2,1,0:T(8,128)}), f32[4,16,512]{2,1,0:T(8,128)S(1)}, u32[]{:S(2)}, u32[]{:S(2)}) async-start(f32[4,16,512]{2,1,0:T(8,128)} %bitcast.64), calls=%async_computation.4 | async-start | bytes 262144 | tf_op jit(solution)/shard_map/all_to_all | solution.py:157
  248.1 5.8 %all-to-all-done.4 = f32[4,16,512]{2,1,0:T(8,128)S(1)} async-done(((f32[4,16,512]{2,1,0:T(8,128)}), f32[4,16,512]{2,1,0:T(8,128)S(1)}, u32[]{:S(2)}, u32[]{:S(2)}) %all-to-all-start.4) | async-done | bytes 131104 | tf_op jit(solution)/shard_map/all_to_all | solution.py:157
  253.9 16.0 %shard_map.105 = (f32[1536,2,1024]{2,1,0:T(2,128)}, f32[1536,2,1024]{2,1,0:T(2,128)}, f32[1536,2,1024]{2,1,0:T(2,128)}, f32[64,256]{1,0:T(8,128)}) custom-call(bf16[1536,2048]{1,0:T(8,128)(2,1)} %copy.43.rows_ref, bf16[2048,256]{1,0:T(8,128)(2,1)} %all-gather.12.cloned.1.call-done.cot_ref, ...), custom_call_target="tpu_custom_call", output_to_operand_aliasing={{0}: (6, {}), {1}: (7, {}), {2}: (8, {})} | custom-call | flops 1610612736 | bytes 15728640 | tf_op jit(solution)/shard_map/pallas_call | solution.py:54
  269.8 3.3 %all-to-all-start.5 = ((f32[4,16,256]{2,1,0:T(8,128)}), f32[4,16,256]{2,1,0:T(8,128)S(1)}, u32[]{:S(2)}, u32[]{:S(2)}) async-start(f32[4,16,256]{2,1,0:T(8,128)} %bitcast.66), calls=%async_computation.5 | async-start | bytes 131072 | tf_op jit(solution)/shard_map/all_to_all | solution.py:157
  273.2 5.7 %all-to-all-done.5 = f32[4,16,256]{2,1,0:T(8,128)S(1)} async-done(((f32[4,16,256]{2,1,0:T(8,128)}), f32[4,16,256]{2,1,0:T(8,128)S(1)}, u32[]{:S(2)}, u32[]{:S(2)}) %all-to-all-start.5) | async-done | bytes 65568 | tf_op jit(solution)/shard_map/all_to_all | solution.py:157
  278.9 0.6 maximum_bitcast_fusion
  (37 shorter events, 0.5 us)
Async XLA Ops:
  7.2 100.4 %copy-start = (bf16[8,6144]{1,0:T(8,128)(2,1)S(1)}, bf16[8,6144]{1,0:T(8,128)(2,1)}, u32[]{:S(2)}) copy-start(bf16[8,6144]{1,0:T(8,128)(2,1)} %param.7) | copy-start | bytes 294916
  7.2 65.8 %all-gather.6.cloned.1.call-start = ((), (), s32[]{:S(2)}) async-start(), calls=%async_computation.6 | async-start | bytes 2621440 | tf_op jit(solution)/shard_map/all_gather | solution.py:139
  10.1 8.5 %slice-start = ((bf16[1,512,2,1024]{3,2,1,0:T(2,128)(2,1)}), bf16[1,512,2,384]{3,2,1,0:T(2,128)(2,1)S(1)}, s32[]{:S(2)}) async-start(bf16[1,512,2,1024]{3,2,1,0:T(2,128)(2,1)} %param.10), calls=%async_computation.10 | async-start | bytes 1572864 | tf_op jit(solution)/shard_map/slice | solution.py:134
  12.3 47.7 %all-to-all-start = ((bf16[64,4,1536]{2,0,1:T(8,128)(2,1)}), bf16[64,4,1536]{2,0,1:T(8,128)(2,1)S(1)}, u32[]{:S(2)}, u32[]{:S(2)}) async-start(bf16[64,4,1536]{2,0,1:T(8,128)(2,1)} %bitcast.40), calls=%async_computation | async-start | bytes 1572864 | tf_op jit(solution)/shard_map/all_to_all | solution.py:141
  18.6 159.6 %all-gather.8.cloned.1.call-start = ((), (), s32[]{:S(2)}) async-start(), calls=%async_computation.7 | async-start | bytes 3932160 | tf_op jit(solution)/shard_map/all_gather | solution.py:146
  73.0 136.5 %all-gather.10.cloned.1.call-start = ((), (), s32[]{:S(2)}) async-start(), calls=%async_computation.8 | async-start | bytes 2621440 | tf_op jit(solution)/shard_map/all_gather | solution.py:146
  73.1 11.1 %collective-permute-start = (bf16[1,1,1,4,64,768]{5,4,3,2,1,0:T(8,128)(2,1)S(1)}, bf16[1,1,1,4,64,768]{5,4,3,2,1,0:T(8,128)(2,1)S(1)}, u32[]{:S(2)}, u32[]{:S(2)}) collective-permute-start(bf16[1,1,1,4,64,768]{5,4,3,2,1,0:T(8,128)(2,1)S(1)} %bitcast.59), channel_id=1, source_target_pairs={{0,8},{4,12},{8,0},{12,4},{16,24},{20,28},{24,16},{28,20},{1,9},{5... | collective-permute-start | bytes 1179656 | tf_op jit(solution)/shard_map/ppermute | solution.py:94
  74.7 12.2 %collective-permute-start.3 = (bf16[1,1,1,4,64,768]{5,4,3,2,1,0:T(8,128)(2,1)S(1)}, bf16[1,1,1,4,64,768]{5,4,3,2,1,0:T(8,128)(2,1)S(1)}, u32[]{:S(2)}, u32[]{:S(2)}) collective-permute-start(bf16[1,1,1,4,64,768]{5,4,3,2,1,0:T(8,128)(2,1)S(1)} %bitcast.57), channel_id=1, source_target_pairs={{0,16},{4,20},{8,24},{12,28},{16,0},{20,4},{24,8},{28,12},{1,17},{... | collective-permute-start | bytes 1179656 | tf_op jit(solution)/shard_map/ppermute | solution.py:94
  84.4 18.8 %collective-permute-start.1 = (bf16[1,2,1,4,64,768]{5,4,3,2,1,0:T(8,128)(2,1)S(1)}, bf16[1,2,1,4,64,768]{5,4,3,2,1,0:T(8,128)(2,1)}, u32[]{:S(2)}, u32[]{:S(2)}) collective-permute-start(bf16[1,2,1,4,64,768]{5,4,3,2,1,0:T(8,128)(2,1)S(1)} %pad_maximum_fusion.5), channel_id=1, source_target_pairs={{0,16},{4,20},{8,24},{12,28},{16,0},{20,4},{24,8},{28,12},{1,17},{... | collective-permute-start | bytes 2359304 | tf_op jit(solution)/shard_map/ppermute | solution.py:94
  87.1 18.6 %collective-permute-start.4 = (bf16[2,1,1,4,64,768]{5,4,3,2,1,0:T(8,128)(2,1)S(1)}, bf16[2,1,1,4,64,768]{5,4,3,2,1,0:T(8,128)(2,1)S(1)}, u32[]{:S(2)}, u32[]{:S(2)}) collective-permute-start(bf16[2,1,1,4,64,768]{5,4,3,2,1,0:T(8,128)(2,1)S(1)} %pad_maximum_fusion.6), channel_id=1, source_target_pairs={{0,8},{4,12},{8,0},{12,4},{16,24},{20,28},{24,16},{28,20},{1,9},{5... | collective-permute-start | bytes 2359304 | tf_op jit(solution)/shard_map/ppermute | solution.py:94
  105.7 1.9 copy-start.3
  105.7 19.3 %collective-permute-start.2 = (bf16[2,2,1,4,64,768]{5,4,3,2,1,0:T(8,128)(2,1)}, bf16[2,2,1,4,64,768]{5,4,3,2,1,0:T(8,128)(2,1)}, u32[]{:S(2)}, u32[]{:S(2)}) collective-permute-start(bf16[2,2,1,4,64,768]{5,4,3,2,1,0:T(8,128)(2,1)} %pad_maximum_fusion.3), channel_id=1, source_target_pairs={{0,4},{4,0},{8,12},{12,8},{16,20},{20,16},{24,28},{28,24},{1,5},{5... | collective-permute-start | bytes 4718600 | tf_op jit(solution)/shard_map/ppermute | solution.py:94
  107.1 17.9 %collective-permute-start.5 = (bf16[2,2,1,4,64,768]{5,4,3,2,1,0:T(8,128)(2,1)}, bf16[2,2,1,4,64,768]{5,4,3,2,1,0:T(8,128)(2,1)}, u32[]{:S(2)}, u32[]{:S(2)}) collective-permute-start(bf16[2,2,1,4,64,768]{5,4,3,2,1,0:T(8,128)(2,1)} %pad_maximum_fusion.4), channel_id=1, source_target_pairs={{0,4},{4,0},{8,12},{12,8},{16,20},{20,16},{24,28},{28,24},{1,5},{5... | collective-permute-start | bytes 4718600 | tf_op jit(solution)/shard_map/ppermute | solution.py:94
  119.6 20.7 %all-to-all-start.1 = ((bf16[16,4,1536]{2,0,1:T(8,128)(2,1)}), bf16[16,4,1536]{2,0,1:T(8,128)(2,1)S(1)}, u32[]{:S(2)}, u32[]{:S(2)}) async-start(bf16[16,4,1536]{2,0,1:T(8,128)(2,1)} %copy.39), calls=%async_computation.1 | async-start | bytes 393216 | tf_op jit(solution)/shard_map/all_to_all | solution.py:125
  123.0 125.1 %all-gather.12.cloned.1.call-start = ((), (), s32[]{:S(2)}) async-start(), calls=%async_computation.9 | async-start | bytes 1310720 | tf_op jit(solution)/shard_map/all_gather | solution.py:146
  140.3 0.7 copy-start.2
  205.3 16.9 %all-to-all-start.3 = ((f32[4,16,768]{2,1,0:T(8,128)}), f32[4,16,768]{2,1,0:T(8,128)S(1)}, u32[]{:S(2)}, u32[]{:S(2)}) async-start(f32[4,16,768]{2,1,0:T(8,128)} %bitcast.63), calls=%async_computation.3 | async-start | bytes 393216 | tf_op jit(solution)/shard_map/all_to_all | solution.py:157
  244.6 9.2 %all-to-all-start.4 = ((f32[4,16,512]{2,1,0:T(8,128)}), f32[4,16,512]{2,1,0:T(8,128)S(1)}, u32[]{:S(2)}, u32[]{:S(2)}) async-start(f32[4,16,512]{2,1,0:T(8,128)} %bitcast.64), calls=%async_computation.4 | async-start | bytes 262144 | tf_op jit(solution)/shard_map/all_to_all | solution.py:157
  253.9 25.6 %copy-start.1 = (bf16[8,6144]{1,0:T(8,128)(2,1)S(1)}, bf16[8,6144]{1,0:T(8,128)(2,1)}, u32[]{:S(2)}) copy-start(bf16[8,6144]{1,0:T(8,128)(2,1)} %param.7) | copy-start | bytes 294916
  269.8 9.0 %all-to-all-start.5 = ((f32[4,16,256]{2,1,0:T(8,128)}), f32[4,16,256]{2,1,0:T(8,128)S(1)}, u32[]{:S(2)}, u32[]{:S(2)}) async-start(f32[4,16,256]{2,1,0:T(8,128)} %bitcast.66), calls=%async_computation.5 | async-start | bytes 131072 | tf_op jit(solution)/shard_map/all_to_all | solution.py:157
Sparse Core Ops, SparseCore 0:
  10.2 62.7 all-gather.5
  74.5 66.7 all-gather.7
  142.9 47.2 all-gather.9
  191.6 31.4 all-gather.11
